TPU v7x, 32 devices: a whole 2x2x4 slice. The times are simulated.
32 devices in a mesh: groups: 2 (over x), dp: 2 (over core), tensor: 8 (over z, y).
Axes of the slice: x: 2, y: 2, z: 4, core: 2. Of those that a mesh axis runs over, the one named last changes fastest.
Arguments:
- reward_hidden: bfloat16 [32, 256, 8192], P(('groups', 'dp'), None, 'tensor'), parts along dimension 0, may hold values from -6 to 6
- reward_gain: float32 [8192], P('tensor'), may hold values from 0.5 to 1.5
- reward_head: float32 [8192], P('tensor'), may hold values from -1 to 1
- decode_inputs: bfloat16 [2, 32, 8192], P(None, ('groups', 'dp'), 'tensor'), parts along dimension 1, may hold values from -6 to 6
- attn_gain: float32 [8192], replicated, may hold values from 0.5 to 1.5
- w_query: bfloat16 [8192, 8192], P(None, 'tensor'), may hold values from -0.0625 to 0.0625
- w_keyval: bfloat16 [8192, 2048], P(None, 'tensor'), may hold values from -0.0625 to 0.0625
- w_out: bfloat16 [8192, 8192], P('tensor'), may hold values from -3 to 3
- cache_keys: bfloat16 [32, 2048, 1024], P(('groups', 'dp'), 'tensor'), parts along dimension 0, may hold values from -720 to 720
- cache_values: bfloat16 [32, 2048, 1024], P(('groups', 'dp'), 'tensor'), parts along dimension 0, may hold values from -6 to 6
- lengths: int32 [32], P('groups'), parts along dimension 0, may hold values from 512 to 2048
- slot_map: int32 [32], P('groups'), parts along dimension 0, may hold values from 0 to 15, as said below
Outputs:
- reward: float32 [32], P(('groups', 'dp')), parts along dimension 0
- decoded: bfloat16 [2, 32, 8192], P(None, ('groups', 'dp'), 'tensor'), parts along dimension 1
There are 2 independent parts, one for each index of `groups`. A program takes and returns all parts, laid end to end along the dimension named above; an argument that names none is the same for every part. Nothing has to cross between parts.
Inputs may be any that keep to these rules, and one draw needn't show every extreme that they name: `slot_map`: each aligned block of 8 slots holds exactly 4 survivors, which map to themselves; every other slot maps to a survivor, and every survivor is named by exactly one other slot.
All inputs are finite; a program needn't handle non-finite values.
Results may differ from a plain program's by a relative error of at most 0.0055.
The roundings to bfloat16 on the way count: a program that leaves them out, or rounds other values in their place, can miss the bound.
Values may be sent and summed in bfloat16 or wider, within the bound.
A program may use at most 128 MiB of HBM per device.

v0:
```python
import jax
import jax.numpy as jnp
from jax import lax
from jax.sharding import PartitionSpec as P

D = 8192
QH = 64
KVH = 8
HD = 128
STEPS = 2


EPS = 1e-05
NEG = -1e30


def fold_sources(parts):
    maxima, totals, sums = parts
    top = jnp.max(maxima, axis=0)
    factor = jnp.exp(maxima - top[None])
    return (top, jnp.sum(factor * totals, axis=0), jnp.sum(factor[..., None] * sums, axis=0))


def local(
    reward_hidden,
    reward_gain,
    reward_head,
    decode_inputs,
    attn_gain,
    w_query,
    w_keyval,
    w_out,
    cache_keys,
    cache_values,
    lengths,
    slot_map,
):
    hidden = reward_hidden.astype(jnp.float32)
    squares = jnp.sum(hidden * hidden, axis=-1)
    head_dot = jnp.sum(hidden * (reward_gain * reward_head), axis=-1)
    squares, head_dot = lax.psum((squares, head_dot), "tensor")
    reward = jnp.mean(head_dot * lax.rsqrt(squares / D + EPS), axis=-1)
    rows = cache_keys.shape[0]
    width = cache_keys.shape[1]
    base = lax.axis_index("dp") * rows
    mine = lax.dynamic_slice_in_dim(slot_map, base, rows)
    every_k, every_v = (
        lax.all_gather(cache_keys, "dp", axis=0, tiled=True),
        lax.all_gather(cache_values, "dp", axis=0, tiled=True),
    )
    keys_now = jnp.take(every_k, mine, axis=0)
    values_now = jnp.take(every_v, mine, axis=0)
    live = jnp.take(lengths, mine, axis=0)
    group = QH // KVH
    heads_dev = w_query.shape[1] // HD
    keys4 = keys_now.reshape(rows, width, KVH, HD)
    values4 = values_now.reshape(rows, width, KVH, HD)
    positions = lax.axis_index("tensor") * width + jnp.arange(width)
    valid = (positions[None, :] < live[:, None])[:, None, None, :]
    head_start = lax.axis_index("tensor") * heads_dev
    kv_index = (head_start + jnp.arange(heads_dev)) // group
    scale = HD ** (-0.5)
    new_keys = []
    new_values = []
    outputs = []
    for step in range(STEPS):
        whole = lax.all_gather(decode_inputs[step], "tensor", axis=1, tiled=True).astype(
            jnp.float32
        )
        normed = (
            whole * lax.rsqrt(jnp.mean(whole * whole, axis=-1, keepdims=True) + EPS) * attn_gain
        ).astype(jnp.bfloat16)
        query_part = jnp.dot(normed, w_query, preferred_element_type=jnp.float32).astype(
            jnp.bfloat16
        )
        kv_part = jnp.dot(normed, w_keyval, preferred_element_type=jnp.float32).astype(jnp.bfloat16)
        query_all, keyval = (
            lax.all_gather(query_part, "tensor", axis=1, tiled=True),
            lax.all_gather(kv_part, "tensor", axis=1, tiled=True),
        )
        query = query_all.reshape(rows, KVH, group, HD)
        keyval = keyval.reshape(rows, 2, KVH, HD)
        new_keys.append(keyval[:, 0])
        new_values.append(keyval[:, 1])
        scores = (
            jnp.einsum("rkgd,rwkd->rkgw", query, keys4, preferred_element_type=jnp.float32) * scale
        )
        scores = jnp.where(valid, scores, NEG)
        block_max = jnp.max(scores, axis=-1)
        expo = jnp.where(valid, jnp.exp(scores - block_max[..., None]), 0.0)
        block_total = jnp.sum(expo, axis=-1).reshape(rows, QH)
        block_acc = jnp.einsum(
            "rkgw,rwkd->rkgd",
            expo.astype(jnp.bfloat16),
            values4,
            preferred_element_type=jnp.float32,
        )
        block_acc = block_acc.reshape(rows, QH, HD)
        block_max = block_max.reshape(rows, QH)
        cache_top, cache_total, cache_acc = fold_sources(
            (
                lax.all_to_all(block_max[None], "tensor", split_axis=2, concat_axis=0, tiled=True),
                lax.all_to_all(
                    block_total[None], "tensor", split_axis=2, concat_axis=0, tiled=True
                ),
                lax.all_to_all(block_acc[None], "tensor", split_axis=2, concat_axis=0, tiled=True),
            )
        )
        query_own = query_part.reshape(rows, heads_dev, HD)
        fresh_k = jnp.take(jnp.stack(new_keys, axis=1), kv_index, axis=2)
        fresh_v = jnp.take(jnp.stack(new_values, axis=1), kv_index, axis=2)
        recent = (
            jnp.einsum("rhd,rjhd->rhj", query_own, fresh_k, preferred_element_type=jnp.float32)
            * scale
        )
        recent_max = jnp.max(recent, axis=-1)
        recent_exp = jnp.exp(recent - recent_max[..., None])
        recent_total = jnp.sum(recent_exp, axis=-1)
        recent_acc = jnp.einsum(
            "rhj,rjhd->rhd",
            recent_exp.astype(jnp.bfloat16),
            fresh_v,
            preferred_element_type=jnp.float32,
        )
        top = jnp.maximum(cache_top, recent_max)
        cache_factor = jnp.exp(cache_top - top)
        recent_factor = jnp.exp(recent_max - top)
        total = cache_factor * cache_total + recent_factor * recent_total
        acc = cache_factor[..., None] * cache_acc + recent_factor[..., None] * recent_acc
        attended = (acc / total[..., None]).astype(jnp.bfloat16).reshape(rows, heads_dev * HD)
        partial_out = jnp.dot(attended, w_out, preferred_element_type=jnp.float32)
        summed = lax.psum_scatter(partial_out, "tensor", scatter_dimension=1, tiled=True)
        outputs.append(summed.astype(jnp.bfloat16))
    return (reward, jnp.stack(outputs, axis=0))


def solution(mesh):
    return jax.shard_map(
        local,
        mesh=mesh,
        in_specs=(
            P(("groups", "dp"), None, "tensor"),
            P("tensor"),
            P("tensor"),
            P(None, ("groups", "dp"), "tensor"),
            P(),
            P(None, "tensor"),
            P(None, "tensor"),
            P("tensor", None),
            P(("groups", "dp"), "tensor", None),
            P(("groups", "dp"), "tensor", None),
            P("groups"),
            P("groups"),
        ),
        out_specs=(P(("groups", "dp")), P(None, ("groups", "dp"), "tensor")),
        check_vma=False,
    )
```

profile of v0, /device:TPU:1, one launch (start us, length us, event | category | flops | bytes accessed | tf_op | source)
XLA Modules:
  0.0 481.4 jit_solution(13673014890106930044)
XLA Ops:
  7.2 0.7 all-gather.5.cloned.1.call-update
  8.0 0.7 all-gather.7.cloned.1.call-update
  8.7 25.6 %all-gather = bf16[1,8,8192]{2,1,0:T(8,128)(2,1)S(1)} all-gather(bf16[1,8,1024]{2,1,0:T(8,128)(2,1)S(1)} %get-tuple-element.26), channel_id=2, replica_groups=mesh['groups'=2,'dp'=2,'tensor'=8] {'tensor'}, dimensions={2}, use_global_device_ids=true | all-gather | bytes 147456 | tf_op jit(solution)/shard_map/all_gather | solution.py:67
  34.4 0.2 fusion.36
  34.5 2.9 convolution_convert_fusion.3
  37.4 24.0 %all_gather.27 = bf16[8,2048]{1,0:T(8,128)(2,1)S(1)} all-gather(bf16[8,256]{1,0:T(8,128)(2,1)S(1)} %convolution_convert_fusion.3), channel_id=1, replica_groups=mesh['groups'=2,'dp'=2,'tensor'=8] {'tensor'}, dimensions={1}, use_global_device_ids=true | all-gather | bytes 36864 | tf_op jit(solution)/shard_map/all_gather | solution.py:79
  61.5 0.6 gather_fusion.2
  62.1 8.2 %fusion.61 = (f32[8,8]{0,1:T(8,128)S(1)}, bf16[8,1024]{1,0:T(8,128)(2,1)S(1)}) fusion(bf16[8,8,128]{2,1,0:T(8,128)(2,1)S(1)} %gather_fusion.2, pred[8]{0:T(512)(128)(4,1)S(1)} %compare_and_fusion, bf16[8192,1024]{1,0:T(8,128)(2,1)} %param.23, bf16[1,8,8192]{2,1,0:T(8,128)(2,1)S(1)} %all-gather, f32[8192]{0:T(1024)S(1)} %copy-done.2, f32[8]{0:T(128)S(1)} %add_rsqrt_fusion.1), kind=kOutput, calls=%fused_computation.78 | convolution fusion | flops 134528960 | bytes 16974120 | tf_op jit(solution)/shard_map/dot_general | solution.py:73
  70.3 0.6 gather_fusion.4
  70.9 24.2 %all-gather.1 = bf16[1,8,8192]{2,1,0:T(8,128)(2,1)S(1)} all-gather(bf16[1,8,1024]{2,1,0:T(8,128)(2,1)S(1)} %get-tuple-element.27), channel_id=3, replica_groups=mesh['groups'=2,'dp'=2,'tensor'=8] {'tensor'}, dimensions={2}, use_global_device_ids=true | all-gather | bytes 147456 | tf_op jit(solution)/shard_map/all_gather | solution.py:67
  95.1 0.2 fusion.39
  95.3 2.9 convolution_convert_fusion.2
  98.1 24.1 %all_gather.31 = bf16[8,2048]{1,0:T(8,128)(2,1)S(1)} all-gather(bf16[8,256]{1,0:T(8,128)(2,1)S(1)} %convolution_convert_fusion.2), channel_id=1, replica_groups=mesh['groups'=2,'dp'=2,'tensor'=8] {'tensor'}, dimensions={1}, use_global_device_ids=true | all-gather | bytes 36864 | tf_op jit(solution)/shard_map/all_gather | solution.py:79
  122.3 0.6 gather_fusion.5
  122.8 0.6 gather_fusion.6
  123.5 8.1 %convolution_convert_fusion = bf16[8,1024]{1,0:T(8,128)(2,1)S(1)} fusion(bf16[8192,1024]{1,0:T(8,128)(2,1)} %param.23, bf16[1,8,8192]{2,1,0:T(8,128)(2,1)S(1)} %all-gather.1, f32[8]{0:T(128)S(1)} %add_rsqrt_fusion, f32[8192]{0:T(1024)S(1)} %copy-done.2), kind=kOutput, calls=%fused_computation.31 | convolution fusion | flops 134488064 | bytes 16957472 | tf_op jit(solution)/shard_map/dot_general | solution.py:73
  131.6 0.2 fusion.65
  131.8 0.1 copy.142
  132.0 0.1 copy.134
  132.1 0.1 copy.143
  132.3 0.1 compare_and_fusion.1
  132.4 0.6 gather_fusion
  133.0 3.6 fusion.1
  136.7 30.0 %all-reduce = (f32[8,256]{1,0:T(8,128)S(1)}, f32[8,256]{1,0:T(8,128)S(1)}) all-reduce(f32[8,256]{1,0:T(8,128)S(1)} %get-tuple-element.6, f32[8,256]{1,0:T(8,128)S(1)} %get-tuple-element.4), channel_id=1, replica_groups=mesh['groups'=2,'dp'=2,'tensor'=8] {'tensor'}, use_global_device_ids=true, to_apply=%region_1.0 | all-reduce | flops 4096 | bytes 32768 | tf_op jit(solution)/shard_map/psum | solution.py:41
  166.7 24.3 %all_gather.30 = bf16[8,8192]{1,0:T(8,128)(2,1)S(1)} all-gather(bf16[8,1024]{1,0:T(8,128)(2,1)S(1)} %convolution_convert_fusion), channel_id=1, replica_groups=mesh['groups'=2,'dp'=2,'tensor'=8] {'tensor'}, dimensions={1}, use_global_device_ids=true | all-gather | bytes 147456 | tf_op jit(solution)/shard_map/all_gather | solution.py:78
  191.1 24.3 %all_gather.25 = bf16[8,8192]{1,0:T(8,128)(2,1)S(1)} all-gather(bf16[8,1024]{1,0:T(8,128)(2,1)S(1)} %get-tuple-element.43), channel_id=1, replica_groups=mesh['groups'=2,'dp'=2,'tensor'=8] {'tensor'}, dimensions={1}, use_global_device_ids=true | all-gather | bytes 147456 | tf_op jit(solution)/shard_map/all_gather | solution.py:78
  215.5 0.2 fusion.63
  215.7 6.1 %gather_fusion.1 = bf16[8,256,1024]{2,1,0:T(8,128)(2,1)} fusion(bf16[16,256,1024]{2,1,0:T(8,128)(2,1)} %all-gather.5.cloned.1.call-done, s32[1024]{0:T(1024)S(1)} %pad_clamp_fusion.1), kind=kCustom, calls=%fused_computation.clone | custom fusion | bytes 8388640 | tf_op jit(solution)/shard_map/jit(_take)/gather | solution.py:51
  221.8 6.2 %gather_fusion.3 = bf16[8,256,1024]{2,1,0:T(8,128)(2,1)} fusion(bf16[16,256,1024]{2,1,0:T(8,128)(2,1)} %all-gather.7.cloned.1.call-done, s32[1024]{0:T(1024)S(1)} %pad_clamp_fusion.1), kind=kCustom, calls=%fused_computation.3.clone | custom fusion | bytes 8388640 | tf_op jit(solution)/shard_map/jit(_take)/gather | solution.py:52
  228.0 6.2 %select_bitcast_fusion.1 = (bf16[8,32,8,8,128]{4,3,2,1,0:T(8,128)(2,1)S(1)}, bf16[8,32,8,8,128]{4,3,2,1,0:T(8,128)(2,1)}) fusion(bf16[8,256,1024]{2,1,0:T(8,128)(2,1)} %gather_fusion.1, pred[8]{0:T(512)(128)(4,1)S(1)} %get-tuple-element.18, bf16[8,256,1024]{2,1,0:T(8,128)(2,1)} %gather_fusion.3), kind=kLoop, calls=%fused_computation.20 | loop fusion | flops 4194304 | bytes 16777224
  234.2 1.3 fusion.105
  235.5 1.3 fusion.104
  236.8 0.7 copy.114
  237.5 3.3 all-to-all-start
  240.8 2.9 fusion.26
  243.7 0.4 fusion.32
  244.2 0.7 copy.147
  244.9 1.4 all-to-all-done
  246.3 3.9 all-to-all-start.2
  250.2 2.9 fusion.29
  253.2 0.7 copy.128
  253.9 0.9 copy.118
  254.7 0.7 copy.148
  255.4 0.8 copy.131
  256.3 0.1 copy.115
  256.3 5.4 %all-to-all-start.5 = ((f32[1,8,64]{1,0,2:T(1,128)}), f32[1,8,64]{1,0,2:T(1,128)S(1)}, u32[]{:S(2)}, u32[]{:S(2)}) async-start(f32[1,8,64]{1,0,2:T(1,128)} %bitcast.47), calls=%async_computation.6 | async-start | bytes 65536 | tf_op jit(solution)/shard_map/all_to_all | solution.py:103
  261.8 0.1 copy.124
  261.9 5.4 %all-to-all-done.5 = f32[1,8,64]{1,0,2:T(1,128)S(1)} async-done(((f32[1,8,64]{1,0,2:T(1,128)}), f32[1,8,64]{1,0,2:T(1,128)S(1)}, u32[]{:S(2)}, u32[]{:S(2)}) %all-to-all-start.5) | async-done | bytes 2080 | tf_op jit(solution)/shard_map/all_to_all | solution.py:103
  267.3 3.3 all-to-all-start.3
  270.7 5.4 %all-to-all-done.3 = f32[1,8,64]{1,0,2:T(1,128)S(1)} async-done(((f32[1,8,64]{1,0,2:T(1,128)}), f32[1,8,64]{1,0,2:T(1,128)S(1)}, u32[]{:S(2)}, u32[]{:S(2)}) %all-to-all-start.3) | async-done | bytes 2080 | tf_op jit(solution)/shard_map/all_to_all | solution.py:102
  276.1 3.4 all-to-all-start.1
  279.9 6.7 %all-to-all-done.1 = f32[1,8,64,128]{3,1,0,2:T(8,128)S(1)} async-done(((f32[1,8,64,128]{3,1,0,2:T(8,128)}), f32[1,8,64,128]{3,1,0,2:T(8,128)S(1)}, u32[]{:S(2)}, u32[]{:S(2)}) %all-to-all-start.1) | async-done | bytes 262176 | tf_op jit(solution)/shard_map/all_to_all | solution.py:106
  286.6 3.4 all-to-all-start.4
  290.0 0.1 fusion.44
  290.2 8.8 %fusion.75 = f32[8,8192]{1,0:T(8,128)} fusion(bf16[1024,8192]{1,0:T(8,128)(2,1)} %param.25, f32[8,8,128]{2,1,0:T(8,128)S(1)} %fusion.44, bf16[8,8,128]{2,1,0:T(8,128)(2,1)S(1)} %gather_fusion.4, f32[8,8]{0,1:T(8,128)S(1)} %copy.125, f32[8,8]{0,1:T(8,128)S(1)} %copy.122, f32[8,8]{0,1:T(8,128)S(1)} %copy.121, f32[8,8]{0,1:T(8,128)S(1)} %copy.116, ...), kind=kOutput, calls=%fused_computation.96 | convolution fusion | flops 134283264 | bytes 17089544 | tf_op jit(solution)/shard_map/dot_general | solution.py:131
  299.1 0.1 multiply_reduce_fusion
  299.2 8.8 %fusion.73 = f32[8,8192]{1,0:T(8,128)} fusion(bf16[1024,8192]{1,0:T(8,128)(2,1)} %param.25, f32[8,8,1,128]{3,2,1,0:T(1,128)S(1)} %fusion.63, f32[8,8,128]{2,0,1:T(8,128)S(1)} %multiply_reduce_fusion, f32[8,8]{0,1:T(8,128)S(1)} %get-tuple-element.13, f32[8,8]{0,1:T(8,128)S(1)} %get-tuple-element.15, f32[8,8]{0,1:T(8,128)S(1)} %get-tuple-element.14), kind=kOutput, calls=%fused_computation.94 | convolution fusion | flops 134258688 | bytes 17105664 | tf_op jit(solution)/shard_map/dot_general | solution.py:131
  308.0 0.1 multiply_reduce_fusion.2
  308.1 0.5 broadcast_multiply_fusion
  308.7 100.9 %reduce-scatter.3.cloned.1.call-done = f32[8,1024]{1,0:T(8,128)} async-done(((f32[8,8192]{1,0:T(8,128)}), f32[8,1024]{1,0:T(8,128)}) %reduce-scatter.3.cloned.1.call-update) | async-done | bytes 32784 | tf_op jit(solution)/shard_map/reduce_scatter | solution.py:132
  409.6 0.8 convert_bitcast_fusion.1
  410.3 63.2 %reduce-scatter.5.cloned.1.call-done = f32[8,1024]{1,0:T(8,128)} async-done(((f32[8,8192]{1,0:T(8,128)}), f32[8,1024]{1,0:T(8,128)}) %reduce-scatter.5.cloned.1.call-update) | async-done | bytes 32784 | tf_op jit(solution)/shard_map/reduce_scatter | solution.py:132
  473.5 0.8 convert_bitcast_fusion
  474.3 0.6 pad_maximum_fusion.2
  (53 shorter events, 1.1 us)
Async XLA Ops:
  7.2 125.2 %copy-start = (s32[16]{0:T(128)S(1)}, s32[16]{0:T(128)}, u32[]{:S(2)}) copy-start(s32[16]{0:T(128)} %param.28) | copy-start | bytes 196
  7.2 1.5 copy-start.3
  7.2 27.4 %copy-start.2 = (f32[8192]{0:T(1024)S(1)}, f32[8192]{0:T(1024)}, u32[]{:S(2)}) copy-start(f32[8192]{0:T(1024)} %param.22) | copy-start | bytes 98308
  7.2 208.5 %all-gather.5.cloned.1.call-start = ((), (), s32[]{:S(2)}) async-start(), calls=%async_computation.8 | async-start | bytes 12582912 | tf_op jit(solution)/shard_map/all_gather | solution.py:48
  7.9 213.9 %all-gather.7.cloned.1.call-start = ((), (), s32[]{:S(2)}) async-start(), calls=%async_computation.9 | async-start | bytes 12582912 | tf_op jit(solution)/shard_map/all_gather | solution.py:49
  123.5 8.8 %copy-start.6 = (s32[16]{0:T(128)S(1)}, s32[16]{0:T(128)}, u32[]{:S(2)}) copy-start(s32[16]{0:T(128)} %param.29) | copy-start | bytes 196
  123.5 9.5 %copy-start.4 = (f32[1024]{0:T(1024)S(1)}, f32[1024]{0:T(1024)}, u32[]{:S(2)}) copy-start(f32[1024]{0:T(1024)} %param.19) | copy-start | bytes 12292
  123.5 9.5 %copy-start.5 = (f32[1024]{0:T(1024)S(1)}, f32[1024]{0:T(1024)}, u32[]{:S(2)}) copy-start(f32[1024]{0:T(1024)} %param.20) | copy-start | bytes 12292
  237.5 8.8 %all-to-all-start = ((f32[1,8,64]{1,0,2:T(1,128)}), f32[1,8,64]{1,0,2:T(1,128)S(1)}, u32[]{:S(2)}, u32[]{:S(2)}) async-start(f32[1,8,64]{1,0,2:T(1,128)} %bitcast.3), calls=%async_computation | async-start | bytes 65536 | tf_op jit(solution)/shard_map/all_to_all | solution.py:102
  246.3 10.0 %all-to-all-start.2 = ((f32[1,8,64]{1,0,2:T(1,128)}), f32[1,8,64]{1,0,2:T(1,128)S(1)}, u32[]{:S(2)}, u32[]{:S(2)}) async-start(f32[1,8,64]{1,0,2:T(1,128)} %bitcast.21), calls=%async_computation.2 | async-start | bytes 65536 | tf_op jit(solution)/shard_map/all_to_all | solution.py:103
  256.3 11.0 %all-to-all-start.5 = ((f32[1,8,64]{1,0,2:T(1,128)}), f32[1,8,64]{1,0,2:T(1,128)S(1)}, u32[]{:S(2)}, u32[]{:S(2)}) async-start(f32[1,8,64]{1,0,2:T(1,128)} %bitcast.47), calls=%async_computation.6 | async-start | bytes 65536 | tf_op jit(solution)/shard_map/all_to_all | solution.py:103
  267.3 8.8 %all-to-all-start.3 = ((f32[1,8,64]{1,0,2:T(1,128)}), f32[1,8,64]{1,0,2:T(1,128)S(1)}, u32[]{:S(2)}, u32[]{:S(2)}) async-start(f32[1,8,64]{1,0,2:T(1,128)} %bitcast.30), calls=%async_computation.4 | async-start | bytes 65536 | tf_op jit(solution)/shard_map/all_to_all | solution.py:102
  276.1 10.4 %all-to-all-start.1 = ((f32[1,8,64,128]{3,1,0,2:T(8,128)}), f32[1,8,64,128]{3,1,0,2:T(8,128)S(1)}, u32[]{:S(2)}, u32[]{:S(2)}) async-start(f32[1,8,64,128]{3,1,0,2:T(8,128)} %copy.118), calls=%async_computation.1 | async-start | bytes 524288 | tf_op jit(solution)/shard_map/all_to_all | solution.py:106
  286.6 12.5 %all-to-all-start.4 = ((f32[1,8,64,128]{3,1,0,2:T(8,128)}), f32[1,8,64,128]{3,1,0,2:T(8,128)S(1)}, u32[]{:S(2)}, u32[]{:S(2)}) async-start(f32[1,8,64,128]{3,1,0,2:T(8,128)} %copy.131), calls=%async_computation.5 | async-start | bytes 524288 | tf_op jit(solution)/shard_map/all_to_all | solution.py:106
  290.0 119.6 %reduce-scatter.3.cloned.1.call-start = ((), (), s32[]{:S(2)}) async-start(), calls=%async_computation.10 | async-start | bytes 294912 | tf_op jit(solution)/shard_map/reduce_scatter | solution.py:132
  299.0 174.5 %reduce-scatter.5.cloned.1.call-start = ((), (), s32[]{:S(2)}) async-start(), calls=%async_computation.11 | async-start | bytes 294912 | tf_op jit(solution)/shard_map/reduce_scatter | solution.py:132
  299.2 175.7 %copy-start.1 = (s32[16]{0:T(128)S(1)}, s32[16]{0:T(128)}, u32[]{:S(2)}) copy-start(s32[16]{0:T(128)} %param.28) | copy-start | bytes 196
Sparse Core Ops, SparseCore 0:
  9.6 22.3 all-gather.4
  33.5 21.0 all-gather.6
  299.1 110.4 reduce-scatter.2
  412.8 60.7 reduce-scatter.4
where the time goes:
time: 485 us; the launch traced here: 481 us
  waiting for transfers between devices  185 us (38%)
  blocking collectives  177 us (36%)
  matrix products  48.4 us (10%)
  starting transfers between devices  23 us (5%)
  local copies, waits for them, and re-layouts  20.7 us (4%)
  other arithmetic  14.1 us (3%)
  between operations  14.1 us (3%)
    reduce_scatter x2, waiting for transfers between devices, local(): lax.psum_scatter(partial_out, 'tensor', scatter_dimension=1, tiled=True)  164 us
    all_gather x2, blocking collectives, local(): lax.all_gather(decode_inputs[step], 'tensor', axis=1, tiled=True)  49.8 us
    all_gather x2, blocking collectives, local(): lax.all_gather(query_part, 'tensor', axis=1, tiled=True)  48.6 us
    all_gather x2, blocking collectives, local(): lax.all_gather(kv_part, 'tensor', axis=1, tiled=True)  48.2 us
    psum x1, blocking collectives, local(): squares, head_dot = lax.psum((squares, head_dot), 'tensor')  30 us
    dot_general x2, matrix products, local(): partial_out = jnp.dot(attended, w_out, preferred_element_type=jnp.float32)  17.6 us
    dot_general x2, matrix products, local(): jnp.dot(normed, w_query, preferred_element_type=jnp.float32)  16.2 us
  transfers between devices with their start and end apart: 10, of which 6 were waited for; matrix products, arithmetic and copies ran while one was open for 14% of the time, Pallas kernels for 0%

commit v1 on v0

--- a/solution.py
+++ b/solution.py
@@ -1,6 +1,10 @@
+import functools
+
 import jax
 import jax.numpy as jnp
 from jax import lax
+from jax.experimental import pallas as pl
+from jax.experimental.pallas import tpu as pltpu
 from jax.sharding import PartitionSpec as P
 
 D = 8192
@@ -134,9 +138,418 @@
     return (reward, jnp.stack(outputs, axis=0))
 
 
+def dot(a, b, dims=(((1,), (0,)), ((), ()))):
+    return lax.dot_general(a, b, dims, preferred_element_type=jnp.float32)
+
+
+def iota(shape, dim):
+    return lax.broadcasted_iota(jnp.int32, shape, dim)
+
+
+def kernel(
+    n, ndp, rows, span, width,
+    map_ref, len_ref, x_hbm, gain_ref, rgain_ref, rhead_ref, rh_hbm, wq_hbm, wkv_hbm, wo_hbm, k_hbm, v_hbm,
+    reward_ref, out_ref,
+    rh, wq, wkv, wo, kbuf, vbuf,
+    xall, xg, normed, kvg, qf, qtmp, qsend, qg, accs, accr, mls, mlr, fac, att, osend, orecv, fin, rw,
+    loc, xds, xdr, xs, xr, rs, rr, kvs, kvr, qs, qr, as_, ar, ms, mr, os_, or_, fds, fdr,
+):
+    me = lax.axis_index("tensor")
+    dp = lax.axis_index("dp")
+    other = 1 - dp
+    feat = x_hbm.shape[1]
+    pages = rows // 2
+    per = 2 * STEPS
+    R = rows * STEPS
+    group = QH // KVH
+    unit = group * per
+    total_rows = pages * unit
+    scale = HD ** (-0.5)
+
+    def peer(k):
+        return lax.rem(me + k, n)
+
+    def source(k):
+        return lax.rem(me + n - k, n)
+
+    copies = []
+
+    def load(src, dst):
+        c = pltpu.make_async_copy(src, dst, loc.at[len(copies)])
+        c.start()
+        copies.append(c)
+        return c
+
+    def load_rows(src, dst, parts):
+        step = src.shape[0] // parts
+        return [load(src.at[pl.ds(i * step, step)], dst.at[pl.ds(i * step, step)]) for i in range(parts)]
+
+    c_x = load(x_hbm, xall.at[dp])
+    c_rh = load_rows(rh_hbm, rh, 2)
+    c_wkv = load_rows(wkv_hbm, wkv, 2)
+    c_wq = load_rows(wq_hbm, wq, 4)
+    c_k = load_rows(k_hbm, kbuf, 2)
+    c_v = load_rows(v_hbm, vbuf, 2)
+    c_wo = load_rows(wo_hbm, wo, 4)
+
+    barrier = pltpu.get_barrier_semaphore()
+    for k in range(1, n):
+        pl.semaphore_signal(barrier, inc=1, device_id={"tensor": peer(k)}, device_id_type=pl.DeviceIdType.MESH)
+    pl.semaphore_signal(barrier, inc=1, device_id={"dp": other}, device_id_type=pl.DeviceIdType.MESH)
+
+    def to_peer(k, src, dst, ssem, rsem):
+        return pltpu.make_async_remote_copy(
+            src_ref=src, dst_ref=dst, send_sem=ssem, recv_sem=rsem,
+            device_id={"tensor": peer(k)}, device_id_type=pl.DeviceIdType.MESH,
+        )
+
+    def to_pair(src, dst, ssem, rsem):
+        return pltpu.make_async_remote_copy(
+            src_ref=src, dst_ref=dst, send_sem=ssem, recv_sem=rsem,
+            device_id={"dp": other}, device_id_type=pl.DeviceIdType.MESH,
+        )
+
+    slot = [map_ref[s] for s in range(ndp * rows)]
+    first, second = [], []
+    for b in range(ndp):
+        mine = [jnp.int32(b * rows)] * pages
+        count = jnp.int32(0)
+        for s in range(b * rows, (b + 1) * rows):
+            kept = slot[s] == s
+            for i in range(pages):
+                mine[i] = jnp.where(kept & (count == i), s, mine[i])
+            count = count + jnp.where(kept, 1, 0)
+        first.append(mine)
+        named = []
+        for i in range(pages):
+            found = jnp.int32(0)
+            for s in range(ndp * rows):
+                found = jnp.where((slot[s] == mine[i]) & (mine[i] != s), s, found)
+            named.append(found)
+        second.append(named)
+
+    def own(lists, i):
+        return jnp.where(dp == 0, lists[0][i], lists[1][i])
+
+    first_own = [own(first, i) for i in range(pages)]
+    second_own = [own(second, i) for i in range(pages)]
+
+    c_x.wait()
+    pl.semaphore_wait(barrier, n)
+    pair_x = to_pair(xall.at[dp], xall.at[dp], xds.at[0], xdr.at[0])
+    pair_x.start()
+
+    r_i = iota((R, ndp * R), 0)
+    c_i = iota((R, ndp * R), 1)
+    row_slot = jnp.zeros((R, ndp * R), jnp.int32)
+    for i in range(pages):
+        row_slot = jnp.where(r_i // STEPS == 2 * i, first_own[i], row_slot)
+        row_slot = jnp.where(r_i // STEPS == 2 * i + 1, second_own[i], row_slot)
+    col_slot = (c_i // R) * rows + c_i % rows
+    pick = (row_slot == col_slot) & (r_i % STEPS == (c_i % R) // rows)
+    pick = jnp.where(pick, 1.0, 0.0).astype(jnp.bfloat16)
+
+    pltpu.make_async_remote_copy(
+        src_ref=xall.at[other], dst_ref=xall.at[other], send_sem=xds.at[0], recv_sem=xdr.at[0],
+        device_id={"dp": other}, device_id_type=pl.DeviceIdType.MESH,
+    ).wait_recv()
+    chosen = dot(pick, xall[...].reshape(ndp * R, feat))
+    xg[me] = chosen.astype(jnp.bfloat16)
+    sends = [pair_x]
+    for k in range(1, n):
+        c = to_peer(k, xg.at[me], xg.at[me], xs.at[k], xr.at[k])
+        c.start()
+        sends.append(c)
+
+    for c in c_rh:
+        c.wait()
+    weight = rgain_ref[...] * rhead_ref[...]
+
+    def reward_step(r, carry):
+        start = pl.multiple_of(r * span, span)
+        square = jnp.zeros((span, 128), jnp.float32)
+        head = jnp.zeros((span, 128), jnp.float32)
+        for b in range(feat // 128):
+            h = rh[pl.ds(start, span), b * 128 : (b + 1) * 128].astype(jnp.float32)
+            square = square + h * h
+            head = head + h * weight[:, b * 128 : (b + 1) * 128]
+        rw[0, 0, pl.ds(r, 1), :] = jnp.sum(jnp.transpose(square), axis=0, keepdims=True)
+        rw[0, 1, pl.ds(r, 1), :] = jnp.sum(jnp.transpose(head), axis=0, keepdims=True)
+        return carry
+
+    lax.fori_loop(0, rows, reward_step, 0)
+    for k in range(1, n):
+        c = to_peer(k, rw.at[0], rw.at[k], rs.at[k], rr.at[k])
+        c.start()
+        sends.append(c)
+
+    mean = jnp.zeros((R, 1), jnp.float32)
+    for k in range(n):
+        if k:
+            s = source(k)
+            to_peer(k, xg.at[s], xg.at[s], xs.at[k], xr.at[k]).wait_recv()
+    for s in range(n):
+        part = xg[s].astype(jnp.float32)
+        mean = mean + jnp.sum(part * part, axis=1, keepdims=True)
+    factor = lax.rsqrt(mean / (n * feat) + EPS)
+    for s in range(n):
+        lo, hi = s * feat, (s + 1) * feat
+        part = xg[s].astype(jnp.float32)
+        normed[:, lo:hi] = (part * factor * gain_ref[:, lo:hi]).astype(jnp.bfloat16)
+
+    for c in c_wkv:
+        c.wait()
+    kvg[0] = dot(normed[...], wkv[...]).astype(jnp.bfloat16)
+    kv_cols = wkv.shape[1]
+    for k in range(1, n):
+        c = to_peer(k, kvg.at[0], kvg.at[me + 1], kvs.at[k], kvr.at[k])
+        c.start()
+        sends.append(c)
+    for c in c_wq:
+        c.wait()
+    chunk = 256
+
+    def query_step(c, carry):
+        cols = pl.ds(pl.multiple_of(c * chunk, chunk), chunk)
+        qf[:, cols] = dot(normed[...], wq[:, cols])
+        return carry
+
+    lax.fori_loop(0, group * HD // chunk, query_step, 0)
+    for i in range(pages):
+        for h in range(group):
+            at = i * unit + h * per
+            qtmp[at : at + per, :] = qf[i * per : (i + 1) * per, h * HD : (h + 1) * HD]
+    qsend[...] = qtmp[...].astype(jnp.bfloat16)
+    for k in range(1, n):
+        c = to_peer(k, qsend, qg.at[k], qs.at[k], qr.at[k])
+        c.start()
+        sends.append(c)
+    qg[0] = qsend[...]
+
+    for c in c_k + c_v:
+        c.wait()
+    live = [len_ref[first_own[i]] for i in range(pages)]
+    page = [first_own[i] - dp * rows for i in range(pages)]
+    place = me * width + iota((unit, width), 1)
+    lane = iota((unit, HD), 1)
+
+    def attend(k):
+        cols = pl.ds(pl.multiple_of(source(k) * HD, HD), HD)
+        packed = []
+        for i in range(pages):
+            q = qg[k, i * unit : (i + 1) * unit, :]
+            valid = place < live[i]
+            score = dot(q, kbuf[page[i], :, cols], (((1,), (1,)), ((), ()))) * scale
+            score = jnp.where(valid, score, NEG)
+            top = jnp.max(score, axis=1, keepdims=True)
+            expo = jnp.where(valid, jnp.exp(score - top), 0.0)
+            total = jnp.sum(expo, axis=1, keepdims=True)
+            acc = dot(expo.astype(jnp.bfloat16), vbuf[page[i], :, cols])
+            accs[k, i * unit : (i + 1) * unit, :] = acc.astype(jnp.bfloat16)
+            packed.append(jnp.where(lane == 0, top, jnp.where(lane == 1, total, 0.0)))
+        mls[k] = jnp.transpose(jnp.concatenate(packed, axis=0))[:8]
+
+    def reply(k):
+        dest = {"tensor": source(k)}
+        return [
+            pltpu.make_async_remote_copy(
+                src_ref=accs.at[k], dst_ref=accr.at[k], send_sem=as_.at[k], recv_sem=ar.at[k],
+                device_id=dest, device_id_type=pl.DeviceIdType.MESH,
+            ),
+            pltpu.make_async_remote_copy(
+                src_ref=mls.at[k], dst_ref=mlr.at[k], send_sem=ms.at[k], recv_sem=mr.at[k],
+                device_id=dest, device_id_type=pl.DeviceIdType.MESH,
+            ),
+        ]
+
+    def attend_step(k, carry):
+        to_peer(k, qsend, qg.at[k], qs.at[k], qr.at[k]).wait_recv()
+        attend(k)
+        for c in reply(k):
+            c.start()
+        return carry
+
+    lax.fori_loop(1, n, attend_step, 0)
+    attend(0)
+
+    for k in range(1, n):
+        to_peer(k, kvg.at[0], kvg.at[source(k) + 1], kvs.at[k], kvr.at[k]).wait_recv()
+    kvg[me + 1] = kvg[0]
+    per_dev = kv_cols // HD
+
+    def new_head(index):
+        return kvg[index // per_dev + 1, :, pl.ds(pl.multiple_of((index % per_dev) * HD, HD), HD)]
+
+    fresh_k = new_head(me)
+    fresh_v = new_head(me + KVH)
+    q_row = iota((total_rows, R), 0)
+    k_row = iota((total_rows, R), 1)
+    q_slot = (q_row // unit) * 2 + (q_row % per) // STEPS
+    valid = (q_slot == k_row // STEPS) & (k_row % STEPS <= q_row % STEPS)
+    score = dot(qsend[...], fresh_k, (((1,), (1,)), ((), ()))) * scale
+    score = jnp.where(valid, score, NEG)
+    new_top = jnp.max(score, axis=1, keepdims=True)
+    expo = jnp.where(valid, jnp.exp(score - new_top), 0.0)
+    new_total = jnp.sum(expo, axis=1, keepdims=True)
+    new_acc = dot(expo.astype(jnp.bfloat16), fresh_v)
+    lane = iota((total_rows, HD), 1)
+    new_ml = jnp.transpose(jnp.where(lane == 0, new_top, jnp.where(lane == 1, new_total, 0.0)))
+
+    for k in range(1, n):
+        to_peer(k, rw.at[0], rw.at[k], rs.at[k], rr.at[k]).wait_recv()
+    sums = jnp.sum(rw[...], axis=0)
+    score = sums[1] * lax.rsqrt(sums[0] / (n * feat) + EPS)
+    score = jnp.sum(score, axis=1, keepdims=True) / span
+    diag = iota((rows, rows), 0) == iota((rows, rows), 1)
+    reward_ref[...] = jnp.sum(jnp.where(diag, score, 0.0), axis=0, keepdims=True)
+
+    for k in range(1, n):
+        for c in reply(k):
+            c.wait_recv()
+    tops = [mls[0, 0:1, :]] + [mlr[k, 0:1, :] for k in range(1, n)] + [new_ml[0:1]]
+    totals = [mls[0, 1:2, :]] + [mlr[k, 1:2, :] for k in range(1, n)] + [new_ml[1:2]]
+    top = functools.reduce(jnp.maximum, tops)
+    factors = [jnp.exp(t - top) for t in tops]
+    whole = functools.reduce(jnp.add, [f * t for f, t in zip(factors, totals)])
+    inverse = 1.0 / whole
+    fac[...] = jnp.zeros_like(fac)
+    for k in range(n + 1):
+        fac[k : k + 1, :] = factors[k] * inverse
+    turned = jnp.transpose(fac[...])
+    folded = turned[:, n : n + 1] * new_acc + turned[:, 0:1] * accs[0].astype(jnp.float32)
+    for k in range(1, n):
+        folded = folded + turned[:, k : k + 1] * accr[k].astype(jnp.float32)
+    qtmp[...] = folded
+    for i in range(pages):
+        for h in range(group):
+            at = i * unit + h * per
+            qf[i * per : (i + 1) * per, h * HD : (h + 1) * HD] = qtmp[at : at + per, :]
+    att[...] = qf[...].astype(jnp.bfloat16)
+
+    for c in c_wo:
+        c.wait()
+
+    def out_part(k):
+        return dot(att[...], wo[:, pl.ds(pl.multiple_of(peer(k) * feat, feat), feat)])
+
+    def out_step(k, carry):
+        osend[k] = out_part(k).astype(jnp.bfloat16)
+        to_peer(k, osend.at[k], orecv.at[k], os_.at[k], or_.at[k]).start()
+        return carry
+
+    lax.fori_loop(1, n, out_step, 0)
+    qf[...] = out_part(0)
+    summed = qf[...]
+    for k in range(1, n):
+        to_peer(k, osend.at[k], orecv.at[k], os_.at[k], or_.at[k]).wait_recv()
+        summed = summed + orecv[k].astype(jnp.float32)
+    fin[dp] = summed.astype(jnp.bfloat16)
+    pair_f = to_pair(fin.at[dp], fin.at[dp], fds.at[0], fdr.at[0])
+    pair_f.start()
+    sends.append(pair_f)
+
+    virtual = jnp.zeros((R, ndp * R), jnp.int32)
+    for b in range(ndp):
+        for i in range(pages):
+            at = b * rows + 2 * i
+            virtual = jnp.where(c_i // STEPS == at, first[b][i], virtual)
+            virtual = jnp.where(c_i // STEPS == at + 1, second[b][i], virtual)
+    place_back = (virtual == dp * rows + r_i % rows) & (c_i % STEPS == r_i // rows)
+    place_back = jnp.where(place_back, 1.0, 0.0).astype(jnp.bfloat16)
+    pltpu.make_async_remote_copy(
+        src_ref=fin.at[other], dst_ref=fin.at[other], send_sem=fds.at[0], recv_sem=fdr.at[0],
+        device_id={"dp": other}, device_id_type=pl.DeviceIdType.MESH,
+    ).wait_recv()
+    out_ref[...] = dot(place_back, fin[...].reshape(ndp * R, feat)).astype(jnp.bfloat16)
+
+    for c in sends:
+        c.wait_send()
+    for k in range(1, n):
+        for c in reply(k):
+            c.wait_send()
+        to_peer(k, osend.at[k], orecv.at[k], os_.at[k], or_.at[k]).wait_send()
+
+
+def fused(
+    n, ndp,
+    reward_hidden, reward_gain, reward_head, decode_inputs, attn_gain, w_query, w_keyval, w_out,
+    cache_keys, cache_values, lengths, slot_map,
+):
+    rows, span, feat = reward_hidden.shape
+    width = cache_keys.shape[1]
+    R = STEPS * rows
+    cols = w_query.shape[1]
+    kv_cols = w_keyval.shape[1]
+    bf, f32 = jnp.bfloat16, jnp.float32
+    total_rows = rows * STEPS * (QH // KVH)
+    big = [
+        pltpu.VMEM((rows * span, feat), bf),
+        pltpu.VMEM(w_query.shape, bf),
+        pltpu.VMEM(w_keyval.shape, bf),
+        pltpu.VMEM(w_out.shape, bf),
+        pltpu.VMEM(cache_keys.shape, bf),
+        pltpu.VMEM(cache_values.shape, bf),
+    ]
+    small = [
+        pltpu.VMEM((ndp, R, feat), bf),
+        pltpu.VMEM((n, R, feat), bf),
+        pltpu.VMEM((R, n * feat), bf),
+        pltpu.VMEM((n + 1, R, kv_cols), bf),
+        pltpu.VMEM((R, cols), f32),
+        pltpu.VMEM((total_rows, HD), f32),
+        pltpu.VMEM((total_rows, HD), bf),
+        pltpu.VMEM((n, total_rows, HD), bf),
+        pltpu.VMEM((n, total_rows, HD), bf),
+        pltpu.VMEM((n, total_rows, HD), bf),
+        pltpu.VMEM((n, 8, total_rows), f32),
+        pltpu.VMEM((n, 8, total_rows), f32),
+        pltpu.VMEM((HD, total_rows), f32),
+        pltpu.VMEM((R, cols), bf),
+        pltpu.VMEM((n, R, feat), bf),
+        pltpu.VMEM((n, R, feat), bf),
+        pltpu.VMEM((ndp, R, feat), bf),
+        pltpu.VMEM((n, 2, rows, span), f32),
+    ]
+    sem = pltpu.SemaphoreType.DMA
+    sems = [sem((17,)), sem((1,)), sem((1,))] + [sem((n,)) for _ in range(14)] + [sem((1,)), sem((1,))]
+    vmem, smem, hbm = (pl.BlockSpec(memory_space=m) for m in (pltpu.VMEM, pltpu.SMEM, pl.ANY))
+    reward, out = pl.pallas_call(
+        functools.partial(kernel, n, ndp, rows, span, width),
+        out_shape=(jax.ShapeDtypeStruct((1, rows), f32), jax.ShapeDtypeStruct((R, feat), bf)),
+        in_specs=[smem, smem, hbm, vmem, vmem, vmem] + [hbm] * 6,
+        out_specs=(vmem, vmem),
+        scratch_shapes=big + small + sems,
+        compiler_params=pltpu.CompilerParams(
+            collective_id=0, has_side_effects=True, vmem_limit_bytes=60 * 2**20
+        ),
+        name="prune_and_decode",
+    )(
+        slot_map,
+        lengths,
+        decode_inputs.reshape(R, feat),
+        attn_gain.reshape(1, -1),
+        reward_gain.reshape(1, -1),
+        reward_head.reshape(1, -1),
+        reward_hidden.reshape(rows * span, feat),
+        w_query,
+        w_keyval,
+        w_out,
+        cache_keys,
+        cache_values,
+    )
+    return reward.reshape(rows), out.reshape(STEPS, rows, feat)
+
+
+def device_program(mesh):
+    n, ndp = mesh.shape["tensor"], mesh.shape["dp"]
+    if n == KVH and ndp == 2:
+        return functools.partial(fused, n, ndp)
+    return local
+
+
 def solution(mesh):
     return jax.shard_map(
-        local,
+        device_program(mesh),
         mesh=mesh,
         in_specs=(
             P(("groups", "dp"), None, "tensor"),

time: 485 us -> 49.5 us (0.10)
  waiting for transfers between devices: 185 us -> 0 us
  blocking collectives: 177 us -> 0 us
  matrix products: 48.4 us -> 0 us
  Pallas kernels: 0 us -> 46 us
  starting transfers between devices: 23 us -> 0 us
  local copies, waits for them, and re-layouts: 20.7 us -> 2.55 us
  other arithmetic: 14.1 us -> 0 us
  between operations: 14.1 us -> 0.64 us
    reduce_scatter x2 -> x0, waiting for transfers between devices: 164 us -> none  [local(): lax.psum_scatter(partial_out, 'tensor', scatter_dimension=1, tiled=True)]
    all_gather x6 -> x0, blocking collectives: 147 us -> none  [the longest x2 49.8 us: local(): lax.all_gather(decode_inputs[step], 'tensor', axis=1, tiled=True)]
    dot_general x12 -> x0, matrix products: 48.4 us -> none  [the longest x2 17.6 us: local(): partial_out = jnp.dot(attended, w_out, preferred_element_type=jnp.float32)]
    pallas_call x0 -> x1, Pallas kernels: none -> 46 us  [fused(): pl.pallas_call(functools.partial(kernel, n, ndp, rows, span, width), out_...]
    psum x1 -> x0, blocking collectives: 30 us -> none  [local(): squares, head_dot = lax.psum((squares, head_dot), 'tensor')]
    all_to_all x6 -> x0, starting transfers between devices: 22.9 us -> none  [the longest x2 9.39 us: local(): lax.all_to_all(block_total[None], 'tensor', split_axis=2, concat_axis=0,...]
    all_to_all x6 -> x0, waiting for transfers between devices: 19 us -> none  [the longest x2 6.88 us: local(): lax.all_to_all(block_max[None], 'tensor', split_axis=2, concat_axis=0, ti...]
    gather x7 -> x0, local copies, waits for them, and re-layouts: 15.2 us -> none  [the longest x1 6.17 us: local(): values_now = jnp.take(every_v, mine, axis=0)]
  transfers between devices with their start and end apart: 10 -> 0, of which waited for: 6 -> 0; matrix products, arithmetic and copies ran while one was open for 14% -> 0% of each run, Pallas kernels for 0% -> 0%
where the time goes in v1:
time: 49.5 us; the launch traced here: 49.2 us
  Pallas kernels  46 us (93%)
  local copies, waits for them, and re-layouts  2.55 us (5%)
  between operations  0.64 us (1%)
    pallas_call x1, Pallas kernels, fused(): pl.pallas_call(functools.partial(kernel, n, ndp, rows, span, width), out_...  46 us
    unnamed x2, local copies, waits for them, and re-layouts  2.55 us

profile of v1, /device:TPU:1, one launch (start us, length us, event | category | flops | bytes accessed | tf_op | source)
XLA Modules:
  0.0 49.2 jit_solution(16800079069366578005)
XLA Ops:
  0.6 46.0 %prune_and_decode.1 = (f32[1,8]{1,0:T(1,128)}, bf16[16,1024]{1,0:T(8,128)(2,1)}) custom-call(s32[16]{0:T(128)} %map_ref.1, s32[16]{0:T(128)} %len_ref.1, bf16[16,1024]{1,0:T(8,128)(2,1)} %bitcast.8, f32[1,8192]{1,0:T(1,128)} %bitcast.9, f32[1,1024]{1,0:T(1,128)} %bitcast.11, f32[1,1024]{1,0:T(1,128)} %bitcast.12, bf16[2048,1024]{1,0:T(8,128)(2,1)} %bitcast.7, ...), custom_call_target="tpu_custom_call" | custom-call | tf_op jit(solution)/shard_map/prune_and_decode/pallas_call | solution.py:516
  46.6 1.2 %copy.16 = f32[8]{0:T(128)} copy(f32[8]{0:T(128)} %bitcast.13) | data formatting | bytes 64
  47.8 1.4 %copy.17 = bf16[2,8,1024]{2,1,0:T(8,128)(2,1)} copy(bf16[2,8,1024]{2,1,0:T(8,128)(2,1)} %bitcast.10) | data formatting | bytes 65536

commit v2 on v1

--- a/solution.py
+++ b/solution.py
@@ -151,8 +151,9 @@
     map_ref, len_ref, x_hbm, gain_ref, rgain_ref, rhead_ref, rh_hbm, wq_hbm, wkv_hbm, wo_hbm, k_hbm, v_hbm,
     reward_ref, out_ref,
     rh, wq, wkv, wo, kbuf, vbuf,
-    xall, xg, normed, kvg, qf, qtmp, qsend, qg, accs, accr, mls, mlr, fac, att, osend, orecv, fin, rw,
-    loc, xds, xdr, xs, xr, rs, rr, kvs, kvr, qs, qr, as_, ar, ms, mr, os_, or_, fds, fdr,
+    xall, xg, normed, kvg, fresh, qf, qtmp, qsend, qg, accs, accr, mls, mlr, fac, att, osend, orecv, fin,
+    rw, rwr, rwo,
+    loc, xds, xdr, xs, xr, rs, rr, rbs, rbr, kvs, kvr, qs, qr, as_, ar, ms, mr, os_, or_, fds, fdr,
 ):
     me = lax.axis_index("tensor")
     dp = lax.axis_index("dp")
@@ -169,8 +170,20 @@
     def peer(k):
         return lax.rem(me + k, n)
 
-    def source(k):
-        return lax.rem(me + n - k, n)
+    nz = n // 2
+    y = lax.rem(me, 2)
+    z = me // 2
+    mate = me + 1 - 2 * y
+
+    def ahead(k):
+        return lax.rem(z + k, nz) * 2 + y
+
+    def ahead_mate(k):
+        return lax.rem(z + k, nz) * 2 + 1 - y
+
+    def source(j):
+        side = j // nz
+        return lax.rem(z + nz - lax.rem(j, nz), nz) * 2 + y + side * (1 - 2 * y)
 
     copies = []
 
@@ -201,6 +214,12 @@
         return pltpu.make_async_remote_copy(
             src_ref=src, dst_ref=dst, send_sem=ssem, recv_sem=rsem,
             device_id={"tensor": peer(k)}, device_id_type=pl.DeviceIdType.MESH,
+        )
+
+    def to_dev(dev, src, dst, ssem, rsem):
+        return pltpu.make_async_remote_copy(
+            src_ref=src, dst_ref=dst, send_sem=ssem, recv_sem=rsem,
+            device_id={"tensor": dev}, device_id_type=pl.DeviceIdType.MESH,
         )
 
     def to_pair(src, dst, ssem, rsem):
@@ -256,10 +275,13 @@
     chosen = dot(pick, xall[...].reshape(ndp * R, feat))
     xg[me] = chosen.astype(jnp.bfloat16)
     sends = [pair_x]
-    for k in range(1, n):
-        c = to_peer(k, xg.at[me], xg.at[me], xs.at[k], xr.at[k])
+    for k in range(1, nz):
+        c = to_dev(ahead(k), xg.at[me], xg.at[me], xs.at[k], xr.at[k])
         c.start()
         sends.append(c)
+    c = to_dev(mate, xg.at[me], xg.at[me], xs.at[nz], xr.at[nz])
+    c.start()
+    sends.append(c)
 
     for c in c_rh:
         c.wait()
@@ -273,21 +295,28 @@
             h = rh[pl.ds(start, span), b * 128 : (b + 1) * 128].astype(jnp.float32)
             square = square + h * h
             head = head + h * weight[:, b * 128 : (b + 1) * 128]
-        rw[0, 0, pl.ds(r, 1), :] = jnp.sum(jnp.transpose(square), axis=0, keepdims=True)
-        rw[0, 1, pl.ds(r, 1), :] = jnp.sum(jnp.transpose(head), axis=0, keepdims=True)
+        rw[r, 0:1, :] = jnp.sum(jnp.transpose(square), axis=0, keepdims=True)
+        rw[r, 1:2, :] = jnp.sum(jnp.transpose(head), axis=0, keepdims=True)
         return carry
 
-    lax.fori_loop(0, rows, reward_step, 0)
-    for k in range(1, n):
-        c = to_peer(k, rw.at[0], rw.at[k], rs.at[k], rr.at[k])
+    lax.fori_loop(0, rows // 2, reward_step, 0)
+    for k in range(1, nz):
+        s = source(k)
+        to_dev(mate, xg.at[s], xg.at[s], xs.at[k], xr.at[k]).wait_recv()
+        c = to_dev(mate, xg.at[s], xg.at[s], xs.at[nz + k], xr.at[nz + k])
         c.start()
         sends.append(c)
+    lax.fori_loop(rows // 2, rows, reward_step, 0)
+    for k in range(1, n):
+        c = to_peer(k, rw.at[peer(k)], rwr.at[k], rs.at[k], rr.at[k])
+        c.start()
+        sends.append(c)
+    rwr[0] = rw[me]
 
     mean = jnp.zeros((R, 1), jnp.float32)
-    for k in range(n):
-        if k:
-            s = source(k)
-            to_peer(k, xg.at[s], xg.at[s], xs.at[k], xr.at[k]).wait_recv()
+    for j in range(nz, n):
+        s = source(j)
+        to_dev(mate, xg.at[s], xg.at[s], xs.at[j], xr.at[j]).wait_recv()
     for s in range(n):
         part = xg[s].astype(jnp.float32)
         mean = mean + jnp.sum(part * part, axis=1, keepdims=True)
@@ -299,12 +328,21 @@
 
     for c in c_wkv:
         c.wait()
-    kvg[0] = dot(normed[...], wkv[...]).astype(jnp.bfloat16)
-    kv_cols = wkv.shape[1]
-    for k in range(1, n):
-        c = to_peer(k, kvg.at[0], kvg.at[me + 1], kvs.at[k], kvr.at[k])
-        c.start()
-        sends.append(c)
+    keyval = dot(normed[...], wkv[...]).astype(jnp.bfloat16)
+    per_dev = wkv.shape[1] // HD
+    kind = me * per_dev // KVH
+    for p in range(per_dev):
+        kvg[p] = keyval[:, p * HD : (p + 1) * HD]
+        dest = lax.rem(me * per_dev + p, KVH)
+
+        @pl.when(dest != me)
+        def _():
+            to_dev(dest, kvg.at[p], fresh.at[kind], kvs.at[p], kvr.at[kind]).start()
+
+        @pl.when(dest == me)
+        def _():
+            fresh[kind] = kvg[p]
+
     for c in c_wq:
         c.wait()
     chunk = 256
@@ -320,10 +358,13 @@
             at = i * unit + h * per
             qtmp[at : at + per, :] = qf[i * per : (i + 1) * per, h * HD : (h + 1) * HD]
     qsend[...] = qtmp[...].astype(jnp.bfloat16)
-    for k in range(1, n):
-        c = to_peer(k, qsend, qg.at[k], qs.at[k], qr.at[k])
+    for k in range(1, nz):
+        c = to_dev(ahead(k), qsend, qg.at[k], qs.at[k], qr.at[k])
         c.start()
         sends.append(c)
+    c = to_dev(mate, qsend, qg.at[nz], qs.at[nz], qr.at[nz])
+    c.start()
+    sends.append(c)
     qg[0] = qsend[...]
 
     for c in c_k + c_v:
@@ -362,26 +403,50 @@
             ),
         ]
 
-    def attend_step(k, carry):
-        to_peer(k, qsend, qg.at[k], qs.at[k], qr.at[k]).wait_recv()
+    def arrived(j):
+        to_dev(mate, qsend, qg.at[j], qs.at[j], qr.at[j]).wait_recv()
+
+    def hand_on(k):
+        return to_dev(mate, qg.at[k], qg.at[nz + k], qs.at[nz + k], qr.at[nz + k])
+
+    def near_step(k, carry):
+        arrived(k)
+        hand_on(k).start()
         attend(k)
         for c in reply(k):
             c.start()
         return carry
 
-    lax.fori_loop(1, n, attend_step, 0)
+    def far_step(j, carry):
+        arrived(j)
+        attend(j)
+        for c in reply(j):
+            c.start()
+        return carry
+
     attend(0)
-
-    for k in range(1, n):
-        to_peer(k, kvg.at[0], kvg.at[source(k) + 1], kvs.at[k], kvr.at[k]).wait_recv()
-    kvg[me + 1] = kvg[0]
-    per_dev = kv_cols // HD
-
-    def new_head(index):
-        return kvg[index // per_dev + 1, :, pl.ds(pl.multiple_of((index % per_dev) * HD, HD), HD)]
-
-    fresh_k = new_head(me)
-    fresh_v = new_head(me + KVH)
+    lax.fori_loop(1, nz, near_step, 0)
+    lax.fori_loop(nz, n, far_step, 0)
+
+    for k in range(1, n):
+        to_peer(k, rw.at[0], rwr.at[k], rs.at[k], rr.at[k]).wait_recv()
+    sums = jnp.sum(rwr[...], axis=0)
+    score = sums[1:2] * lax.rsqrt(sums[0:1] / (n * feat) + EPS)
+    rwo[me] = jnp.broadcast_to(jnp.sum(score, axis=1, keepdims=True) / span, rwo.shape[1:])
+    for k in range(1, n):
+        c = to_peer(k, rwo.at[me], rwo.at[me], rbs.at[k], rbr.at[k])
+        c.start()
+        sends.append(c)
+
+    for kd in range(2):
+        origin = (me + kd * KVH) // per_dev
+
+        @pl.when(origin != me)
+        def _():
+            to_dev(mate, kvg.at[0], fresh.at[kd], kvs.at[0], kvr.at[kd]).wait_recv()
+
+    fresh_k = fresh[0]
+    fresh_v = fresh[1]
     q_row = iota((total_rows, R), 0)
     k_row = iota((total_rows, R), 1)
     q_slot = (q_row // unit) * 2 + (q_row % per) // STEPS
@@ -394,14 +459,6 @@
     new_acc = dot(expo.astype(jnp.bfloat16), fresh_v)
     lane = iota((total_rows, HD), 1)
     new_ml = jnp.transpose(jnp.where(lane == 0, new_top, jnp.where(lane == 1, new_total, 0.0)))
-
-    for k in range(1, n):
-        to_peer(k, rw.at[0], rw.at[k], rs.at[k], rr.at[k]).wait_recv()
-    sums = jnp.sum(rw[...], axis=0)
-    score = sums[1] * lax.rsqrt(sums[0] / (n * feat) + EPS)
-    score = jnp.sum(score, axis=1, keepdims=True) / span
-    diag = iota((rows, rows), 0) == iota((rows, rows), 1)
-    reward_ref[...] = jnp.sum(jnp.where(diag, score, 0.0), axis=0, keepdims=True)
 
     for k in range(1, n):
         for c in reply(k):
@@ -429,19 +486,36 @@
     for c in c_wo:
         c.wait()
 
-    def out_part(k):
-        return dot(att[...], wo[:, pl.ds(pl.multiple_of(peer(k) * feat, feat), feat)])
-
-    def out_step(k, carry):
-        osend[k] = out_part(k).astype(jnp.bfloat16)
-        to_peer(k, osend.at[k], orecv.at[k], os_.at[k], or_.at[k]).start()
+    def out_part(dev):
+        return dot(att[...], wo[:, pl.ds(pl.multiple_of(dev * feat, feat), feat)])
+
+    def mate_share(j):
+        return to_dev(mate, osend.at[j], orecv.at[j], os_.at[j], or_.at[j])
+
+    def pair_share(k):
+        return to_dev(ahead(k), osend.at[k], orecv.at[k], os_.at[k], or_.at[k])
+
+    def mate_step(i, carry):
+        k = lax.rem(i, nz)
+        osend[nz + k] = out_part(ahead_mate(k)).astype(jnp.bfloat16)
+        mate_share(nz + k).start()
         return carry
 
-    lax.fori_loop(1, n, out_step, 0)
-    qf[...] = out_part(0)
+    def pair_step(k, carry):
+        share = out_part(ahead(k))
+        mate_share(nz + k).wait_recv()
+        osend[k] = (share + orecv[nz + k].astype(jnp.float32)).astype(jnp.bfloat16)
+        pair_share(k).start()
+        return carry
+
+    lax.fori_loop(1, nz + 1, mate_step, 0)
+    lax.fori_loop(1, nz, pair_step, 0)
+    qf[...] = out_part(me)
     summed = qf[...]
-    for k in range(1, n):
-        to_peer(k, osend.at[k], orecv.at[k], os_.at[k], or_.at[k]).wait_recv()
+    mate_share(nz).wait_recv()
+    summed = summed + orecv[nz].astype(jnp.float32)
+    for k in range(1, nz):
+        pair_share(k).wait_recv()
         summed = summed + orecv[k].astype(jnp.float32)
     fin[dp] = summed.astype(jnp.bfloat16)
     pair_f = to_pair(fin.at[dp], fin.at[dp], fds.at[0], fdr.at[0])
@@ -462,12 +536,42 @@
     ).wait_recv()
     out_ref[...] = dot(place_back, fin[...].reshape(ndp * R, feat)).astype(jnp.bfloat16)
 
+    result = jnp.zeros((1, rows), jnp.float32)
+    for k in range(1, n):
+        dev = source(k)
+        to_peer(k, rwo.at[me], rwo.at[dev], rbs.at[k], rbr.at[k]).wait_recv()
+    for r in range(rows):
+        result = jnp.where(iota((1, rows), 1) == r, rwo[r, 0:1, 0:rows], result)
+    reward_ref[...] = result
+
     for c in sends:
         c.wait_send()
+    for p in range(per_dev):
+        dest = lax.rem(me * per_dev + p, KVH)
+
+        @pl.when(dest != me)
+        def _():
+            to_dev(dest, kvg.at[p], fresh.at[kind], kvs.at[p], kvr.at[kind]).wait_send()
+
     for k in range(1, n):
         for c in reply(k):
             c.wait_send()
-        to_peer(k, osend.at[k], orecv.at[k], os_.at[k], or_.at[k]).wait_send()
+    for k in range(1, nz):
+        hand_on(k).wait_send()
+        pair_share(k).wait_send()
+    for j in range(nz, n):
+        mate_share(j).wait_send()
+
+
+def write_results(reward_in, out_in, reward_ref, out_ref, sem):
+    copies = [
+        pltpu.make_async_copy(reward_in, reward_ref, sem.at[0]),
+        pltpu.make_async_copy(out_in, out_ref, sem.at[1]),
+    ]
+    for c in copies:
+        c.start()
+    for c in copies:
+        c.wait()
 
 
 def fused(
@@ -494,7 +598,8 @@
         pltpu.VMEM((ndp, R, feat), bf),
         pltpu.VMEM((n, R, feat), bf),
         pltpu.VMEM((R, n * feat), bf),
-        pltpu.VMEM((n + 1, R, kv_cols), bf),
+        pltpu.VMEM((kv_cols // HD, R, HD), bf),
+        pltpu.VMEM((2, R, HD), bf),
         pltpu.VMEM((R, cols), f32),
         pltpu.VMEM((total_rows, HD), f32),
         pltpu.VMEM((total_rows, HD), bf),
@@ -508,10 +613,12 @@
         pltpu.VMEM((n, R, feat), bf),
         pltpu.VMEM((n, R, feat), bf),
         pltpu.VMEM((ndp, R, feat), bf),
-        pltpu.VMEM((n, 2, rows, span), f32),
+        pltpu.VMEM((rows, 2, span), f32),
+        pltpu.VMEM((n, 2, span), f32),
+        pltpu.VMEM((rows, 8, 128), f32),
     ]
     sem = pltpu.SemaphoreType.DMA
-    sems = [sem((17,)), sem((1,)), sem((1,))] + [sem((n,)) for _ in range(14)] + [sem((1,)), sem((1,))]
+    sems = [sem((17,)), sem((1,)), sem((1,))] + [sem((n,)) for _ in range(16)] + [sem((1,)), sem((1,))]
     vmem, smem, hbm = (pl.BlockSpec(memory_space=m) for m in (pltpu.VMEM, pltpu.SMEM, pl.ANY))
     reward, out = pl.pallas_call(
         functools.partial(kernel, n, ndp, rows, span, width),
@@ -537,14 +644,26 @@
         cache_keys,
         cache_values,
     )
+    reward, out = pl.pallas_call(
+        write_results,
+        out_shape=(jax.ShapeDtypeStruct((1, rows), f32), jax.ShapeDtypeStruct((R, feat), bf)),
+        in_specs=[hbm, hbm],
+        out_specs=(hbm, hbm),
+        scratch_shapes=[sem((2,))],
+        name="write_results",
+    )(reward, out)
     return reward.reshape(rows), out.reshape(STEPS, rows, feat)
 
 
 def device_program(mesh):
     n, ndp = mesh.shape["tensor"], mesh.shape["dp"]
-    if n == KVH and ndp == 2:
-        return functools.partial(fused, n, ndp)
-    return local
+
+    def run(*args):
+        if n == KVH and ndp == 2 and args[0].shape[0] == n:
+            return fused(n, ndp, *args)
+        return local(*args)
+
+    return run
 
 
 def solution(mesh):

time: 49.5 us -> 47.5 us (0.960)
  local copies, waits for them, and re-layouts: 2.55 us -> 0 us
  Pallas kernels: 46 us -> 46.7 us
    unnamed x2 -> x0, local copies, waits for them, and re-layouts: 2.55 us -> none
    pallas_call x0 -> x1, Pallas kernels: none -> 2.13 us  [fused(): pl.pallas_call(write_results, out_shape=(jax.ShapeDtypeStruct((1, rows),...]
    pallas_call x1, Pallas kernels: 46 us -> 44.6 us  [fused(): pl.pallas_call(functools.partial(kernel, n, ndp, rows, span, width), out_...]
where the time goes in v2:
time: 47.5 us; the launch traced here: 47.4 us
  Pallas kernels  46.7 us (98%)
  between operations  0.64 us (1%)
    pallas_call x1, Pallas kernels, fused(): pl.pallas_call(functools.partial(kernel, n, ndp, rows, span, width), out_...  44.6 us
    pallas_call x1, Pallas kernels, fused(): pl.pallas_call(write_results, out_shape=(jax.ShapeDtypeStruct((1, rows),...  2.13 us

profile of v2, /device:TPU:1, one launch (start us, length us, event | category | flops | bytes accessed | tf_op | source)
XLA Modules:
  0.0 47.4 jit_solution(3477190224475152671)
XLA Ops:
  0.6 44.6 %prune_and_decode.1 = (f32[1,8]{1,0:T(1,128)}, bf16[16,1024]{1,0:T(8,128)(2,1)}) custom-call(s32[16]{0:T(128)} %map_ref.1, s32[16]{0:T(128)} %len_ref.1, bf16[16,1024]{1,0:T(8,128)(2,1)} %bitcast.8, f32[1,8192]{1,0:T(1,128)} %bitcast.9, f32[1,1024]{1,0:T(1,128)} %bitcast.10, f32[1,1024]{1,0:T(1,128)} %bitcast.11, bf16[2048,1024]{1,0:T(8,128)(2,1)} %bitcast.7, ...), custom_call_target="tpu_custom_call" | custom-call | tf_op jit(solution)/shard_map/prune_and_decode/pallas_call | solution.py:623
  45.2 2.1 %write_results.1 = (f32[1,8]{1,0:T(1,128)}, bf16[16,1024]{1,0:T(8,128)(2,1)}) custom-call(f32[1,8]{1,0:T(1,128)} %get-tuple-element.6.reward_in, bf16[16,1024]{1,0:T(8,128)(2,1)} %get-tuple-element.7.out_in), custom_call_target="tpu_custom_call" | custom-call | tf_op jit(solution)/shard_map/write_results/pallas_call | solution.py:647

commit v3 on v2

--- a/solution.py
+++ b/solution.py
@@ -151,9 +151,9 @@
     map_ref, len_ref, x_hbm, gain_ref, rgain_ref, rhead_ref, rh_hbm, wq_hbm, wkv_hbm, wo_hbm, k_hbm, v_hbm,
     reward_ref, out_ref,
     rh, wq, wkv, wo, kbuf, vbuf,
-    xall, xg, normed, kvg, fresh, qf, qtmp, qsend, qg, accs, accr, mls, mlr, fac, att, osend, orecv, fin,
+    xg, normed, kvg, fresh, qf, qtmp, hq, qhalf, attf, qsend, qg, accs, accr, mls, mlr, fac, att, osend, orecv, hfin, fin,
     rw, rwr, rwo,
-    loc, xds, xdr, xs, xr, rs, rr, rbs, rbr, kvs, kvr, qs, qr, as_, ar, ms, mr, os_, or_, fds, fdr,
+    loc, xps, xpr, xs, xr, rs, rr, rbs, rbr, kvs, kvr, qs, qr, as_, ar, ms, mr, os_, or_, fds, fdr, hqs, hqr, ats, atr,
 ):
     me = lax.axis_index("tensor")
     dp = lax.axis_index("dp")
@@ -197,13 +197,18 @@
         step = src.shape[0] // parts
         return [load(src.at[pl.ds(i * step, step)], dst.at[pl.ds(i * step, step)]) for i in range(parts)]
 
-    c_x = load(x_hbm, xall.at[dp])
+    c_x = load(x_hbm, xg.at[dp, me])
     c_rh = load_rows(rh_hbm, rh, 2)
     c_wkv = load_rows(wkv_hbm, wkv, 2)
-    c_wq = load_rows(wq_hbm, wq, 4)
+    half = wq.shape[1]
+    c_wq = load_rows(wq_hbm.at[:, pl.ds(pl.multiple_of(dp * half, half), half)], wq, 4)
     c_k = load_rows(k_hbm, kbuf, 2)
     c_v = load_rows(v_hbm, vbuf, 2)
-    c_wo = load_rows(wo_hbm, wo, 4)
+    out_half = feat // ndp
+    c_wo = [
+        load(wo_hbm.at[:, pl.ds(pl.multiple_of(s * feat + dp * out_half, out_half), out_half)], wo.at[s])
+        for s in range(n)
+    ]
 
     barrier = pltpu.get_barrier_semaphore()
     for k in range(1, n):
@@ -255,8 +260,17 @@
 
     c_x.wait()
     pl.semaphore_wait(barrier, n)
-    pair_x = to_pair(xall.at[dp], xall.at[dp], xds.at[0], xdr.at[0])
-    pair_x.start()
+    sends = []
+
+    def pass_on(s, j):
+        return to_pair(xg.at[dp, s], xg.at[dp, s], xps.at[j], xpr.at[j])
+
+    def hand_x(dev, s, j):
+        return to_dev(dev, xg.at[dp, s], xg.at[dp, s], xs.at[j], xr.at[j])
+
+    for c in [hand_x(ahead(k), me, k) for k in range(1, nz)] + [hand_x(mate, me, nz), pass_on(me, 0)]:
+        c.start()
+        sends.append(c)
 
     r_i = iota((R, ndp * R), 0)
     c_i = iota((R, ndp * R), 1)
@@ -268,20 +282,21 @@
     pick = (row_slot == col_slot) & (r_i % STEPS == (c_i % R) // rows)
     pick = jnp.where(pick, 1.0, 0.0).astype(jnp.bfloat16)
 
-    pltpu.make_async_remote_copy(
-        src_ref=xall.at[other], dst_ref=xall.at[other], send_sem=xds.at[0], recv_sem=xdr.at[0],
-        device_id={"dp": other}, device_id_type=pl.DeviceIdType.MESH,
-    ).wait_recv()
-    chosen = dot(pick, xall[...].reshape(ndp * R, feat))
-    xg[me] = chosen.astype(jnp.bfloat16)
-    sends = [pair_x]
-    for k in range(1, nz):
-        c = to_dev(ahead(k), xg.at[me], xg.at[me], xs.at[k], xr.at[k])
-        c.start()
-        sends.append(c)
-    c = to_dev(mate, xg.at[me], xg.at[me], xs.at[nz], xr.at[nz])
-    c.start()
-    sends.append(c)
+    r_i = iota((ndp * R, ndp * R), 0)
+    c_i = iota((ndp * R, ndp * R), 1)
+    by_row = jnp.zeros(r_i.shape, jnp.int32)
+    by_col = jnp.zeros(r_i.shape, jnp.int32)
+    for b in range(ndp):
+        for i in range(pages):
+            at = b * rows + 2 * i
+            by_row = jnp.where(r_i // STEPS == at, first[b][i], by_row)
+            by_row = jnp.where(r_i // STEPS == at + 1, second[b][i], by_row)
+            by_col = jnp.where(c_i // STEPS == at, first[b][i], by_col)
+            by_col = jnp.where(c_i // STEPS == at + 1, second[b][i], by_col)
+    pick_all = (by_row == (c_i // R) * rows + c_i % rows) & (r_i % STEPS == (c_i % R) // rows)
+    pick_all = jnp.where(pick_all, 1.0, 0.0).astype(jnp.bfloat16)
+    put_all = (by_col == (r_i // R) * rows + r_i % rows) & (c_i % STEPS == (r_i % R) // rows)
+    put_all = jnp.where(put_all, 1.0, 0.0).astype(jnp.bfloat16)
 
     for c in c_rh:
         c.wait()
@@ -302,10 +317,10 @@
     lax.fori_loop(0, rows // 2, reward_step, 0)
     for k in range(1, nz):
         s = source(k)
-        to_dev(mate, xg.at[s], xg.at[s], xs.at[k], xr.at[k]).wait_recv()
-        c = to_dev(mate, xg.at[s], xg.at[s], xs.at[nz + k], xr.at[nz + k])
-        c.start()
-        sends.append(c)
+        hand_x(mate, s, k).wait_recv()
+        for c in (hand_x(mate, s, nz + k), pass_on(s, k)):
+            c.start()
+            sends.append(c)
     lax.fori_loop(rows // 2, rows, reward_step, 0)
     for k in range(1, n):
         c = to_peer(k, rw.at[peer(k)], rwr.at[k], rs.at[k], rr.at[k])
@@ -313,22 +328,29 @@
         sends.append(c)
     rwr[0] = rw[me]
 
-    mean = jnp.zeros((R, 1), jnp.float32)
     for j in range(nz, n):
         s = source(j)
-        to_dev(mate, xg.at[s], xg.at[s], xs.at[j], xr.at[j]).wait_recv()
+        hand_x(mate, s, j).wait_recv()
+        c = pass_on(s, j)
+        c.start()
+        sends.append(c)
+    for j in range(n):
+        s = source(j)
+        to_pair(xg.at[other, s], xg.at[other, s], xps.at[j], xpr.at[j]).wait_recv()
+    mean = jnp.zeros((ndp * R, 1), jnp.float32)
     for s in range(n):
-        part = xg[s].astype(jnp.float32)
+        part = xg[:, s].reshape(ndp * R, feat).astype(jnp.float32)
         mean = mean + jnp.sum(part * part, axis=1, keepdims=True)
     factor = lax.rsqrt(mean / (n * feat) + EPS)
     for s in range(n):
         lo, hi = s * feat, (s + 1) * feat
-        part = xg[s].astype(jnp.float32)
+        part = xg[:, s].reshape(ndp * R, feat).astype(jnp.float32)
         normed[:, lo:hi] = (part * factor * gain_ref[:, lo:hi]).astype(jnp.bfloat16)
 
     for c in c_wkv:
         c.wait()
     keyval = dot(normed[...], wkv[...]).astype(jnp.bfloat16)
+    keyval = dot(pick, keyval).astype(jnp.bfloat16)
     per_dev = wkv.shape[1] // HD
     kind = me * per_dev // KVH
     for p in range(per_dev):
@@ -352,12 +374,26 @@
         qf[:, cols] = dot(normed[...], wq[:, cols])
         return carry
 
-    lax.fori_loop(0, group * HD // chunk, query_step, 0)
+    lax.fori_loop(0, half // chunk, query_step, 0)
+    qf[...] = dot(pick_all, qf[...].astype(jnp.bfloat16))
+    heads = half // HD
+    small = heads * per
+    for b in range(ndp):
+        for i in range(pages):
+            for h in range(heads):
+                at = i * small + h * per
+                row = b * R + i * per
+                qtmp[at : at + per, :] = qf[row : row + per, h * HD : (h + 1) * HD]
+        hq[b] = qtmp[0 : pages * small, :].astype(jnp.bfloat16)
+    swap_q = to_pair(hq.at[other], qhalf.at[dp], hqs.at[0], hqr.at[0])
+    swap_q.start()
+    sends.append(swap_q)
+    qhalf[dp] = hq[dp]
+    to_pair(hq.at[other], qhalf.at[other], hqs.at[0], hqr.at[0]).wait_recv()
     for i in range(pages):
-        for h in range(group):
-            at = i * unit + h * per
-            qtmp[at : at + per, :] = qf[i * per : (i + 1) * per, h * HD : (h + 1) * HD]
-    qsend[...] = qtmp[...].astype(jnp.bfloat16)
+        for b in range(ndp):
+            at = i * unit + b * small
+            qsend[at : at + small, :] = qhalf[b, i * small : (i + 1) * small, :]
     for k in range(1, nz):
         c = to_dev(ahead(k), qsend, qg.at[k], qs.at[k], qr.at[k])
         c.start()
@@ -480,14 +516,18 @@
     for i in range(pages):
         for h in range(group):
             at = i * unit + h * per
-            qf[i * per : (i + 1) * per, h * HD : (h + 1) * HD] = qtmp[at : at + per, :]
-    att[...] = qf[...].astype(jnp.bfloat16)
+            attf[i * per : (i + 1) * per, h * HD : (h + 1) * HD] = qtmp[at : at + per, :]
+    att[dp] = attf[...].astype(jnp.bfloat16)
+    swap_a = to_pair(att.at[dp], att.at[dp], ats.at[0], atr.at[0])
+    swap_a.start()
+    sends.append(swap_a)
+    to_pair(att.at[other], att.at[other], ats.at[0], atr.at[0]).wait_recv()
 
     for c in c_wo:
         c.wait()
 
     def out_part(dev):
-        return dot(att[...], wo[:, pl.ds(pl.multiple_of(dev * feat, feat), feat)])
+        return dot(att[...].reshape(ndp * R, att.shape[2]), wo[dev])
 
     def mate_share(j):
         return to_dev(mate, osend.at[j], orecv.at[j], os_.at[j], or_.at[j])
@@ -510,31 +550,21 @@
 
     lax.fori_loop(1, nz + 1, mate_step, 0)
     lax.fori_loop(1, nz, pair_step, 0)
-    qf[...] = out_part(me)
-    summed = qf[...]
+    summed = out_part(me)
     mate_share(nz).wait_recv()
     summed = summed + orecv[nz].astype(jnp.float32)
     for k in range(1, nz):
         pair_share(k).wait_recv()
         summed = summed + orecv[k].astype(jnp.float32)
-    fin[dp] = summed.astype(jnp.bfloat16)
-    pair_f = to_pair(fin.at[dp], fin.at[dp], fds.at[0], fdr.at[0])
+    placed = dot(put_all, summed.astype(jnp.bfloat16)).astype(jnp.bfloat16)
+    hfin[...] = placed.reshape(ndp, R, out_half)
+    pair_f = to_pair(hfin.at[other], fin.at[dp], fds.at[0], fdr.at[0])
     pair_f.start()
     sends.append(pair_f)
-
-    virtual = jnp.zeros((R, ndp * R), jnp.int32)
+    fin[dp] = hfin[dp]
+    to_pair(hfin.at[other], fin.at[other], fds.at[0], fdr.at[0]).wait_recv()
     for b in range(ndp):
-        for i in range(pages):
-            at = b * rows + 2 * i
-            virtual = jnp.where(c_i // STEPS == at, first[b][i], virtual)
-            virtual = jnp.where(c_i // STEPS == at + 1, second[b][i], virtual)
-    place_back = (virtual == dp * rows + r_i % rows) & (c_i % STEPS == r_i // rows)
-    place_back = jnp.where(place_back, 1.0, 0.0).astype(jnp.bfloat16)
-    pltpu.make_async_remote_copy(
-        src_ref=fin.at[other], dst_ref=fin.at[other], send_sem=fds.at[0], recv_sem=fdr.at[0],
-        device_id={"dp": other}, device_id_type=pl.DeviceIdType.MESH,
-    ).wait_recv()
-    out_ref[...] = dot(place_back, fin[...].reshape(ndp * R, feat)).astype(jnp.bfloat16)
+        out_ref[:, b * out_half : (b + 1) * out_half] = fin[b]
 
     result = jnp.zeros((1, rows), jnp.float32)
     for k in range(1, n):
@@ -588,20 +618,22 @@
     total_rows = rows * STEPS * (QH // KVH)
     big = [
         pltpu.VMEM((rows * span, feat), bf),
-        pltpu.VMEM(w_query.shape, bf),
+        pltpu.VMEM((n * feat, cols // ndp), bf),
         pltpu.VMEM(w_keyval.shape, bf),
-        pltpu.VMEM(w_out.shape, bf),
+        pltpu.VMEM((n, w_out.shape[0], feat // ndp), bf),
         pltpu.VMEM(cache_keys.shape, bf),
         pltpu.VMEM(cache_values.shape, bf),
     ]
     small = [
-        pltpu.VMEM((ndp, R, feat), bf),
-        pltpu.VMEM((n, R, feat), bf),
-        pltpu.VMEM((R, n * feat), bf),
+        pltpu.VMEM((ndp, n, R, feat), bf),
+        pltpu.VMEM((ndp * R, n * feat), bf),
         pltpu.VMEM((kv_cols // HD, R, HD), bf),
         pltpu.VMEM((2, R, HD), bf),
+        pltpu.VMEM((ndp * R, cols // ndp), f32),
+        pltpu.VMEM((total_rows, HD), f32),
+        pltpu.VMEM((ndp, total_rows // ndp, HD), bf),
+        pltpu.VMEM((ndp, total_rows // ndp, HD), bf),
         pltpu.VMEM((R, cols), f32),
-        pltpu.VMEM((total_rows, HD), f32),
         pltpu.VMEM((total_rows, HD), bf),
         pltpu.VMEM((n, total_rows, HD), bf),
         pltpu.VMEM((n, total_rows, HD), bf),
@@ -609,16 +641,17 @@
         pltpu.VMEM((n, 8, total_rows), f32),
         pltpu.VMEM((n, 8, total_rows), f32),
         pltpu.VMEM((HD, total_rows), f32),
-        pltpu.VMEM((R, cols), bf),
-        pltpu.VMEM((n, R, feat), bf),
-        pltpu.VMEM((n, R, feat), bf),
-        pltpu.VMEM((ndp, R, feat), bf),
+        pltpu.VMEM((ndp, R, cols), bf),
+        pltpu.VMEM((n, ndp * R, feat // ndp), bf),
+        pltpu.VMEM((n, ndp * R, feat // ndp), bf),
+        pltpu.VMEM((ndp, R, feat // ndp), bf),
+        pltpu.VMEM((ndp, R, feat // ndp), bf),
         pltpu.VMEM((rows, 2, span), f32),
         pltpu.VMEM((n, 2, span), f32),
         pltpu.VMEM((rows, 8, 128), f32),
     ]
     sem = pltpu.SemaphoreType.DMA
-    sems = [sem((17,)), sem((1,)), sem((1,))] + [sem((n,)) for _ in range(16)] + [sem((1,)), sem((1,))]
+    sems = [sem((13 + n,))] + [sem((n,)) for _ in range(18)] + [sem((1,)) for _ in range(6)]
     vmem, smem, hbm = (pl.BlockSpec(memory_space=m) for m in (pltpu.VMEM, pltpu.SMEM, pl.ANY))
     reward, out = pl.pallas_call(
         functools.partial(kernel, n, ndp, rows, span, width),

time: 47.5 us -> 49.3 us (1.038)
  Pallas kernels: 46.7 us -> 48.5 us
    pallas_call x1, Pallas kernels: 44.6 us -> 46.3 us  [fused(): pl.pallas_call(functools.partial(kernel, n, ndp, rows, span, width), out_...]
where the time goes in v3:
time: 49.3 us; the launch traced here: 49.1 us
  Pallas kernels  48.5 us (98%)
  between operations  0.64 us (1%)
    pallas_call x1, Pallas kernels, fused(): pl.pallas_call(functools.partial(kernel, n, ndp, rows, span, width), out_...  46.3 us
    pallas_call x1, Pallas kernels, fused(): pl.pallas_call(write_results, out_shape=(jax.ShapeDtypeStruct((1, rows),...  2.13 us

profile of v3, /device:TPU:1, one launch (start us, length us, event | category | flops | bytes accessed | tf_op | source)
XLA Modules:
  0.0 49.1 jit_solution(5405578542213586090)
XLA Ops:
  0.6 46.3 %prune_and_decode.1 = (f32[1,8]{1,0:T(1,128)}, bf16[16,1024]{1,0:T(8,128)(2,1)}) custom-call(s32[16]{0:T(128)} %map_ref.1, s32[16]{0:T(128)} %len_ref.1, bf16[16,1024]{1,0:T(8,128)(2,1)} %bitcast.8, f32[1,8192]{1,0:T(1,128)} %bitcast.9, f32[1,1024]{1,0:T(1,128)} %bitcast.10, f32[1,1024]{1,0:T(1,128)} %bitcast.11, bf16[2048,1024]{1,0:T(8,128)(2,1)} %bitcast.7, ...), custom_call_target="tpu_custom_call" | custom-call | tf_op jit(solution)/shard_map/prune_and_decode/pallas_call | solution.py:656
  47.0 2.1 %write_results.1 = (f32[1,8]{1,0:T(1,128)}, bf16[16,1024]{1,0:T(8,128)(2,1)}) custom-call(f32[1,8]{1,0:T(1,128)} %get-tuple-element.6.reward_in, bf16[16,1024]{1,0:T(8,128)(2,1)} %get-tuple-element.7.out_in), custom_call_target="tpu_custom_call" | custom-call | tf_op jit(solution)/shard_map/write_results/pallas_call | solution.py:680

commit v4 on v2

--- a/solution.py
+++ b/solution.py
@@ -199,11 +199,7 @@
 
     c_x = load(x_hbm, xall.at[dp])
     c_rh = load_rows(rh_hbm, rh, 2)
-    c_wkv = load_rows(wkv_hbm, wkv, 2)
     c_wq = load_rows(wq_hbm, wq, 4)
-    c_k = load_rows(k_hbm, kbuf, 2)
-    c_v = load_rows(v_hbm, vbuf, 2)
-    c_wo = load_rows(wo_hbm, wo, 4)
 
     barrier = pltpu.get_barrier_semaphore()
     for k in range(1, n):
@@ -326,25 +322,12 @@
         part = xg[s].astype(jnp.float32)
         normed[:, lo:hi] = (part * factor * gain_ref[:, lo:hi]).astype(jnp.bfloat16)
 
-    for c in c_wkv:
-        c.wait()
-    keyval = dot(normed[...], wkv[...]).astype(jnp.bfloat16)
-    per_dev = wkv.shape[1] // HD
-    kind = me * per_dev // KVH
-    for p in range(per_dev):
-        kvg[p] = keyval[:, p * HD : (p + 1) * HD]
-        dest = lax.rem(me * per_dev + p, KVH)
-
-        @pl.when(dest != me)
-        def _():
-            to_dev(dest, kvg.at[p], fresh.at[kind], kvs.at[p], kvr.at[kind]).start()
-
-        @pl.when(dest == me)
-        def _():
-            fresh[kind] = kvg[p]
-
     for c in c_wq:
         c.wait()
+    c_wkv = load_rows(wkv_hbm, wkv, 2)
+    c_k = load_rows(k_hbm, kbuf, 2)
+    c_v = load_rows(v_hbm, vbuf, 2)
+    c_wo = load_rows(wo_hbm, wo, 4)
     chunk = 256
 
     def query_step(c, carry):
@@ -366,6 +349,24 @@
     c.start()
     sends.append(c)
     qg[0] = qsend[...]
+
+    for c in c_wkv:
+        c.wait()
+    keyval = dot(normed[...], wkv[...]).astype(jnp.bfloat16)
+    per_dev = wkv.shape[1] // HD
+    kind = me * per_dev // KVH
+    for p in range(per_dev):
+        kvg[p] = keyval[:, p * HD : (p + 1) * HD]
+        dest = lax.rem(me * per_dev + p, KVH)
+
+        @pl.when(dest != me)
+        def _():
+            to_dev(dest, kvg.at[p], fresh.at[kind], kvs.at[p], kvr.at[kind]).start()
+
+        @pl.when(dest == me)
+        def _():
+            fresh[kind] = kvg[p]
+
 
     for c in c_k + c_v:
         c.wait()

time: 47.5 us -> 46.8 us (0.985)
  Pallas kernels: 46.7 us -> 46 us
    pallas_call x1, Pallas kernels: 44.6 us -> 43.8 us  [fused(): pl.pallas_call(functools.partial(kernel, n, ndp, rows, span, width), out_...]
where the time goes in v4:
time: 46.8 us; the launch traced here: 46.6 us
  Pallas kernels  46 us (98%)
  between operations  0.64 us (1%)
    pallas_call x1, Pallas kernels, fused(): pl.pallas_call(functools.partial(kernel, n, ndp, rows, span, width), out_...  43.8 us
    pallas_call x1, Pallas kernels, fused(): pl.pallas_call(write_results, out_shape=(jax.ShapeDtypeStruct((1, rows),...  2.13 us

profile of v4, /device:TPU:1, one launch (start us, length us, event | category | flops | bytes accessed | tf_op | source)
XLA Modules:
  0.0 46.6 jit_solution(15852428050036886279)
XLA Ops:
  0.6 43.8 %prune_and_decode.1 = (f32[1,8]{1,0:T(1,128)}, bf16[16,1024]{1,0:T(8,128)(2,1)}) custom-call(s32[16]{0:T(128)} %map_ref.1, s32[16]{0:T(128)} %len_ref.1, bf16[16,1024]{1,0:T(8,128)(2,1)} %bitcast.8, f32[1,8192]{1,0:T(1,128)} %bitcast.9, f32[1,1024]{1,0:T(1,128)} %bitcast.10, f32[1,1024]{1,0:T(1,128)} %bitcast.11, bf16[2048,1024]{1,0:T(8,128)(2,1)} %bitcast.7, ...), custom_call_target="tpu_custom_call" | custom-call | tf_op jit(solution)/shard_map/prune_and_decode/pallas_call | solution.py:624
  44.5 2.1 %write_results.1 = (f32[1,8]{1,0:T(1,128)}, bf16[16,1024]{1,0:T(8,128)(2,1)}) custom-call(f32[1,8]{1,0:T(1,128)} %get-tuple-element.6.reward_in, bf16[16,1024]{1,0:T(8,128)(2,1)} %get-tuple-element.7.out_in), custom_call_target="tpu_custom_call" | custom-call | tf_op jit(solution)/shard_map/write_results/pallas_call | solution.py:648
